TPU v7x, 512 devices: a whole 4x8x8 slice. The times are simulated.
512 devices in a mesh: tgt: 64 (over y, z), sec: 8 (over x, core).
Axes of the slice: x: 4, y: 8, z: 8, core: 2. Of those that a mesh axis runs over, the one named last changes fastest.
Arguments:
- hidden: bfloat16 [384, 16384], P(None, ('sec', 'tgt'))
- norm_gain: bfloat16 [16384], P('sec'), may hold values from 0.5 to 1.5
- vocab_weight: bfloat16 [16384, 65536], P('sec', 'tgt'), may hold values from -0.125 to 0.125
- draft_gain: bfloat16 [16384], replicated, may hold values from 0.5 to 1.5
- query_weight: bfloat16 [16384, 8192], P('sec', 'tgt'), may hold values from -0.046875 to 0.046875
- draft_tokens: int32 [64, 6], P('sec'), may hold values from 0 to 65535
- accepted: int32 [64], P('sec'), may hold values from 0 to 6
- cache_lengths: int32 [64], P('sec'), may hold values from 0 to 1018
Outputs:
- draft_logprob: float32 [64, 6], P('sec')
- draft_query: bfloat16 [384, 8192], P('sec', 'tgt')
Inputs may be any that keep to these rules, and one draw needn't show every extreme that they name: cache_lengths[r] + p stays below 1024 for every draft position p.
All inputs are finite; a program needn't handle non-finite values.
Results may differ from a plain program's by a relative error of at most 0.0075.
Values may be sent and summed in bfloat16 or wider, within the bound.
A program may use at most 64 MiB of HBM per device.

v0:
```python
import jax
import jax.numpy as jnp
from jax import lax
from jax.sharding import PartitionSpec as P

D = 16384
HD = 128


def rotate_rows(query, cache_lengths, accepted, head_size, positions_each):
    row_count = query.shape[0]
    heads_here = query.shape[1] // head_size
    query = query.reshape(row_count, heads_here, head_size)
    half_size = head_size // 2
    frequency = jnp.power(
        jnp.float32(500000.0), -jnp.arange(half_size, dtype=jnp.float32) * 2.0 / head_size
    )
    positions = (
        cache_lengths[:, None] + jnp.arange(positions_each, dtype=jnp.int32)[None, :]
    ).reshape(-1)
    angles = positions.astype(jnp.float32)[:, None] * frequency[None, :]
    cosine = jnp.cos(angles)[:, None, :]
    sine = jnp.sin(angles)[:, None, :]
    first_half = query[:, :, :half_size]
    second_half = query[:, :, half_size:]
    rotated = jnp.concatenate(
        [first_half * cosine - second_half * sine, second_half * cosine + first_half * sine], axis=2
    )
    accepted_mask = (
        jnp.arange(positions_each, dtype=jnp.int32)[None, :] < accepted[:, None]
    ).reshape(-1)
    rotated = jnp.where(accepted_mask[:, None, None], rotated, jnp.float32(0.0))
    return rotated.reshape(row_count, heads_here * head_size).astype(jnp.bfloat16)


def local(
    hidden, norm_gain, vocab_weight, draft_gain, query_weight, draft_tokens, accepted, cache_lengths
):
    feature_block = lax.all_gather(hidden, "tgt", axis=1, tiled=True)
    block_values = feature_block.astype(jnp.float32)
    sec_index = lax.axis_index("sec")
    partial_squares = jnp.sum(block_values * block_values, axis=1)
    row_squares = lax.psum(partial_squares, "sec")
    row_scale = lax.rsqrt(row_squares / D + 1e-05)
    normed = (block_values * row_scale[:, None] * norm_gain.astype(jnp.float32)[None, :]).astype(
        jnp.bfloat16
    )
    rows_here = draft_tokens.shape[0] * draft_tokens.shape[1]
    row_start = sec_index * rows_here
    partial_logits = jnp.dot(normed, vocab_weight, preferred_element_type=jnp.float32)
    full_logits = lax.psum(partial_logits.astype(jnp.bfloat16), "sec").astype(jnp.float32)
    own_logits = lax.dynamic_slice_in_dim(full_logits, row_start, rows_here, 0)
    vocab_here = vocab_weight.shape[1]
    vocab_start = lax.axis_index("tgt") * vocab_here
    token_ids = draft_tokens.reshape(-1)
    matches = token_ids[:, None] == (vocab_start + jnp.arange(vocab_here, dtype=jnp.int32))[None, :]
    picked_part = jnp.sum(jnp.where(matches, own_logits, jnp.float32(0.0)), axis=1)
    exp_part = jnp.sum(jnp.exp(own_logits), axis=1)
    exp_total, picked = lax.psum((exp_part, picked_part), "tgt")
    draft_logprob = (picked - jnp.log(exp_total)).reshape(
        draft_tokens.shape[0], draft_tokens.shape[1]
    )
    whole_rows = lax.all_to_all(feature_block, "sec", split_axis=0, concat_axis=1, tiled=True)
    own_scale = lax.dynamic_slice_in_dim(row_scale, row_start, rows_here, 0)
    draft_normed = (
        whole_rows.astype(jnp.float32)
        * own_scale[:, None]
        * draft_gain.astype(jnp.float32)[None, :]
    ).astype(jnp.bfloat16)
    query = jnp.dot(
        draft_normed,
        lax.all_gather(query_weight, "sec", axis=0, tiled=True),
        preferred_element_type=jnp.float32,
    )
    draft_query = rotate_rows(query, cache_lengths, accepted, HD, draft_tokens.shape[1])
    return (draft_logprob, draft_query)


def solution(mesh):
    return jax.shard_map(
        local,
        mesh=mesh,
        in_specs=(
            P(None, ("sec", "tgt")),
            P("sec"),
            P("sec", "tgt"),
            P(),
            P("sec", "tgt"),
            P("sec", None),
            P("sec"),
            P("sec"),
        ),
        out_specs=(P("sec", None), P("sec", "tgt")),
        check_vma=False,
    )
```

profile of v0, /device:TPU:2, one launch (start us, length us, event | category | flops | bytes accessed | tf_op | source)
XLA Modules:
  0.0 343.9 jit_solution(12094404594494667091)
XLA Ops:
  7.2 0.0 all-gather.3.cloned.1.call-start
  7.2 0.7 all-gather.3.cloned.1.call-update
  7.9 0.0 all-reduce.3.cloned.1.call-start
  7.9 0.7 convert_element_type.44
  8.6 89.9 %all-gather.3.cloned.1.call-done = bf16[384,2048]{0,1:T(8,128)(2,1)} async-done(((bf16[384,32]{0,1:T(8,128)(2,1)}), bf16[384,2048]{0,1:T(8,128)(2,1)}) %all-gather.3.cloned.1.call-update) | async-done | bytes 1572880 | tf_op jit(solution)/shard_map/all_gather | solution.py:39
  98.5 1.8 fusion
  100.3 10.0 %psum.28 = f32[384]{0:T(512)S(1)} all-reduce(f32[384]{0:T(512)S(1)} %fusion), channel_id=1, replica_groups=mesh['tgt'=64,'sec'=8] {'sec'}, use_global_device_ids=true, to_apply=%region_1.0 | all-reduce | flops 384 | bytes 3072 | tf_op jit(solution)/shard_map/psum | solution.py:43
  110.3 0.0 copy-start
  110.3 5.6 %fusion.10 = bf16[384,1024]{1,0:T(8,128)(2,1)} fusion(bf16[2048,1024]{1,0:T(8,128)(2,1)} %param.10, bf16[384,2048]{0,1:T(8,128)(2,1)} %all-gather.3.cloned.1.call-done, f32[2048]{0:T(1024)S(1)} %convert_element_type.44, f32[384]{0:T(512)S(1)} %add_rsqrt_fusion), kind=kOutput, calls=%fused_computation.13 | convolution fusion | flops 1614151680 | bytes 6563328 | tf_op jit(solution)/shard_map/dot_general | solution.py:50
  115.9 0.0 all-reduce.3.cloned.1.call-update
  115.9 0.0 all-gather.5.cloned.1.call-start
  116.0 0.7 all-gather.5.cloned.1.call-update
  116.7 0.0 copy-done
  116.7 0.0 copy-start.2
  116.7 0.0 copy-start.1
  116.7 0.0 copy-start.3
  116.7 0.0 copy-start.4
  116.7 1.7 copy.12
  118.4 6.5 %all-to-all-start = ((bf16[8,48,2048]{2,1,0:T(8,128)(2,1)}), bf16[8,48,2048]{2,1,0:T(8,128)(2,1)S(1)}, u32[]{:S(2)}, u32[]{:S(2)}) async-start(bf16[8,48,2048]{2,1,0:T(8,128)(2,1)} %bitcast), calls=%async_computation | async-start | bytes 3145728 | tf_op jit(solution)/shard_map/all_to_all | solution.py:63
  124.9 0.0 copy-done.2
  124.9 0.1 eq.15
  125.0 0.0 copy-done.1
  125.0 0.0 copy-done.3
  125.0 0.1 add_convert_fusion
  125.0 0.1 convert_element_type.54
  125.1 0.0 copy-done.4
  125.1 0.1 iota_compare_fusion
  125.2 0.1 lt.30
  125.3 0.1 dynamic_slice.7
  125.4 61.5 %all-reduce.3.cloned.1.call-done = bf16[384,1024]{1,0:T(8,128)(2,1)} async-done(((bf16[384,1024]{1,0:T(8,128)(2,1)}), bf16[384,1024]{1,0:T(8,128)(2,1)}) %all-reduce.3.cloned.1.call-update) | async-done | bytes 786448 | tf_op jit(solution)/shard_map/psum | solution.py:51
  186.9 1.1 fusion.14
  188.0 144.2 %all-reduce = (f32[48]{0:T(128)S(1)}, f32[48]{0:T(128)S(1)}) all-reduce(f32[48]{0:T(128)S(1)} %get-tuple-element.3, f32[48]{0:T(128)S(1)} %get-tuple-element.2), channel_id=1, replica_groups=mesh['tgt'=64,'sec'=8] {'tgt'}, use_global_device_ids=true, to_apply=%region_4.5 | all-reduce | flops 96 | bytes 768 | tf_op jit(solution)/shard_map/psum | solution.py:59
  332.2 0.7 reshape.162
  332.9 0.0 all-to-all-done
  332.9 0.4 convert_bitcast_fusion
  333.3 0.2 copy.14
  333.5 0.0 all-gather.5.cloned.1.call-done
  333.5 3.0 fusion.13
  336.5 0.2 fusion.21
  336.7 0.7 fusion.24
  (5 shorter events, 0.0 us)
Async XLA Ops:
  7.2 91.3 %all-gather.3.cloned.1.call-start = ((), (), s32[]{:S(2)}) async-start(), calls=%async_computation.1 | async-start | bytes 1597440 | tf_op jit(solution)/shard_map/all_gather | solution.py:39
  7.9 179.0 %all-reduce.3.cloned.1.call-start = ((), (), s32[]{:S(2)}) async-start(), calls=%async_computation.2 | async-start | bytes 1572864 | tf_op jit(solution)/shard_map/psum | solution.py:51
  110.3 6.4 %copy-start = (bf16[384,2048]{0,1:T(8,128)(2,1)S(1)}, bf16[384,2048]{0,1:T(8,128)(2,1)}, u32[]{:S(2)}) copy-start(bf16[384,2048]{0,1:T(8,128)(2,1)} %all-gather.3.cloned.1.call-done) | copy-start | bytes 4718596
  115.9 217.5 %all-gather.5.cloned.1.call-start = ((), (), s32[]{:S(2)}) async-start(), calls=%async_computation.3 | async-start | bytes 4718592 | tf_op jit(solution)/shard_map/all_gather | solution.py:72
  116.7 8.2 %copy-start.2 = (s32[8,6]{1,0:T(8,128)S(1)}, s32[8,6]{1,0:T(8,128)}, u32[]{:S(2)}) copy-start(s32[8,6]{1,0:T(8,128)} %param.13) | copy-start | bytes 580
  116.7 8.2 %copy-start.1 = (bf16[16384]{0:T(1024)(128)(2,1)S(1)}, bf16[16384]{0:T(1024)(128)(2,1)}, u32[]{:S(2)}) copy-start(bf16[16384]{0:T(1024)(128)(2,1)} %param.11) | copy-start | bytes 98308
  116.7 8.2 %copy-start.3 = (s32[8]{0:T(128)S(1)}, s32[8]{0:T(128)}, u32[]{:S(2)}) copy-start(s32[8]{0:T(128)} %param.15) | copy-start | bytes 100
  116.7 8.4 %copy-start.4 = (s32[8]{0:T(128)S(1)}, s32[8]{0:T(128)}, u32[]{:S(2)}) copy-start(s32[8]{0:T(128)} %param.14) | copy-start | bytes 100
  118.4 214.5 %all-to-all-start = ((bf16[8,48,2048]{2,1,0:T(8,128)(2,1)}), bf16[8,48,2048]{2,1,0:T(8,128)(2,1)S(1)}, u32[]{:S(2)}, u32[]{:S(2)}) async-start(bf16[8,48,2048]{2,1,0:T(8,128)(2,1)} %bitcast), calls=%async_computation | async-start | bytes 3145728 | tf_op jit(solution)/shard_map/all_to_all | solution.py:63
Sparse Core Ops, SparseCore 0:
  11.1 87.3 all-gather.2
  116.1 70.7 all-reduce.2
  189.3 37.9 all-gather.4
where the time goes:
time: 344 us
  blocking collectives  154 us (45%)
  waiting for transfers between devices  153 us (44%)
  between operations  13.9 us (4%)
  matrix products  8.63 us (3%)
  starting transfers between devices  6.58 us (2%)
  other arithmetic  4.99 us (1%)
    psum x1, blocking collectives, local(): exp_total, picked = lax.psum((exp_part, picked_part), 'tgt')  144 us
    all_gather x1, waiting for transfers between devices, local(): feature_block = lax.all_gather(hidden, 'tgt', axis=1, tiled=True)  89.9 us
    psum x1, waiting for transfers between devices, local(): lax.psum(partial_logits.astype(jnp.bfloat16), 'sec').astype(jnp.float32)  61.5 us
    psum x1, blocking collectives, local(): row_squares = lax.psum(partial_squares, 'sec')  10 us
  transfers between devices with their start and end apart: 4, of which 2 were waited for; matrix products, arithmetic and copies ran while one was open for 2% of the time, Pallas kernels for 0%

commit v1 on v0

v1 whole, which is shorter than its diff:
```python
import jax
import jax.numpy as jnp
from jax import lax
from jax.experimental import pallas as pl
from jax.experimental.pallas import tpu as pltpu
from jax.sharding import PartitionSpec as P

D = 16384
HD = 128
RING = 8
MESH = pl.DeviceIdType.MESH


def kernel(
    h_hbm, gain_hbm, w_hbm, dgain_hbm, wq_hbm, tok_ref, accepted_ref, length_ref,
    lp_ref, dq_ref,
    ga, gb, raw, wa, wb, acc, part, landed, sq, sq_in, gains, msg1, msg2, in1, in2,
    local_sem, p1s, p1r, p2s, p2r, rs_s, rs_r, sq_s, sq_r, e1s, e1r, e2s, e2r,
):
    tgt = lax.axis_index("tgt")
    sec = lax.axis_index("sec")
    y, z = tgt // RING, tgt % RING
    rows, vocab = 384, w_hbm.shape[1]
    own = rows // RING

    def z_peer(d):
        return (y * RING + (z + d) % RING, sec)

    def y_peer(d):
        return (((y + d) % RING) * RING + z, sec)

    def s_peer(d):
        return (tgt, (sec + d) % RING)

    w_copies = [
        pltpu.make_async_copy(w_hbm, raw.at[:, pl.ds(0, vocab)], local_sem.at[0]),
        pltpu.make_async_copy(wq_hbm, raw.at[:, pl.ds(vocab, HD)], local_sem.at[1]),
        pltpu.make_async_copy(gain_hbm, gains.at[0], local_sem.at[2]),
        pltpu.make_async_copy(dgain_hbm.at[pl.ds(sec * 16, 16)], gains.at[1], local_sem.at[3]),
    ]
    h_copies = [
        pltpu.make_async_copy(h_hbm.at[pl.ds(0, 16)], ga.at[y, z], local_sem.at[4]),
        pltpu.make_async_copy(h_hbm.at[pl.ds(16, 16)], gb.at[z, y], local_sem.at[5]),
    ]
    for c in h_copies + w_copies:
        c.start()

    barrier = pltpu.get_barrier_semaphore()
    for d in range(1, RING):
        for peer in (z_peer(d), y_peer(d), s_peer(d)):
            pl.semaphore_signal(barrier, inc=1, device_id=peer, device_id_type=MESH)
    pl.semaphore_wait(barrier, 3 * (RING - 1))

    first = []
    for d in range(1, RING):
        first.append(pltpu.make_async_remote_copy(
            h_hbm.at[pl.ds(0, 16)], ga.at[y, z], p1s.at[0, d], p1r.at[0, d],
            device_id=z_peer(d), device_id_type=MESH))
        first.append(pltpu.make_async_remote_copy(
            h_hbm.at[pl.ds(16, 16)], gb.at[z, y], p1s.at[1, d], p1r.at[1, d],
            device_id=y_peer(d), device_id_type=MESH))
    for c in first:
        c.start()
    for c in h_copies:
        c.wait()
    for c in first:
        c.wait_recv()

    def ring_copies(s):
        out = []
        for k, (buf, at, peer) in enumerate(((ga, y, y_peer), (gb, z, z_peer))):
            for way in (0, 1):
                step = 1 if way == 0 else -1
                block = (at - step * (s - 1)) % RING if s > 1 else at
                ref = buf.at[block]
                if s == 4:
                    ref = buf.at[block, pl.ds(4 * way, 4)]
                out.append(pltpu.make_async_remote_copy(
                    ref, ref, p2s.at[k, way, s - 1], p2r.at[k, way, s - 1],
                    device_id=peer(step), device_id_type=MESH))
        return out

    second = [ring_copies(s) for s in range(1, 5)]
    for c in second[0]:
        c.start()

    for c in w_copies:
        c.wait()
    gt = jnp.transpose(gains[0].astype(jnp.float32))
    dgt = jnp.transpose(gains[1].astype(jnp.float32))
    for j in range(16):
        span = pl.ds(128 * j, 128)
        left = (raw[span, pl.ds(0, vocab)].astype(jnp.float32) * gt[:, j:j + 1]).astype(jnp.bfloat16)
        right = (raw[span, pl.ds(vocab, HD)].astype(jnp.float32) * dgt[:, j:j + 1]).astype(jnp.bfloat16)
        for i in range(4):
            yy, zz = j // 2, 4 * (j % 2) + i
            for wide, values in ((pl.ds(0, vocab), left), (pl.ds(vocab, HD), right)):
                wa[yy, zz, :, wide] = values[32 * i:32 * i + 16]
                wb[zz, yy, :, wide] = values[32 * i + 16:32 * i + 32]

    def take(h_parts, w_parts, fresh):
        h = jnp.concatenate([v.reshape(128, rows) for v in h_parts], axis=0)
        hf = h.astype(jnp.float32)
        squares = jnp.sum((hf * hf).reshape(32, 8, rows), axis=0)
        sq[...] = squares if fresh else sq[...] + squares
        ht = jnp.transpose(h)
        for n in range(3):
            cols = pl.ds(n * 384, 384)
            w = jnp.concatenate([r[b, :, :, cols].reshape(128, 384) for r, b in w_parts], axis=0)
            prod = jnp.dot(ht, w, preferred_element_type=jnp.float32)
            if fresh:
                acc[:, cols] = prod
            else:
                acc[:, cols] += prod

    take([ga[y], gb[z]], [(wa, y), (wb, z)], True)
    for s in range(1, 4):
        for c in second[s - 1]:
            c.wait_recv()
        for c in second[s]:
            c.start()
        for buf, w, at in ((ga, wa, y), (gb, wb, z)):
            b1, b2 = (at + s) % RING, (at + RING - s) % RING
            take([buf[b1], buf[b2]], [(w, b1), (w, b2)], False)
    for c in second[3]:
        c.wait_recv()
    far_y, far_z = (y + 4) % RING, (z + 4) % RING
    take([ga[far_y], gb[far_z]], [(wa, far_y), (wb, far_z)], False)

    sq_copies, rs_copies = [], []
    sq_in[sec] = sq[...]
    for d in range(1, RING):
        sq_copies.append(pltpu.make_async_remote_copy(
            sq, sq_in.at[sec], sq_s.at[d], sq_r.at[d], device_id=s_peer(d), device_id_type=MESH))
        rs_copies.append(pltpu.make_async_remote_copy(
            part.at[(sec + d) % RING], landed.at[sec], rs_s.at[d], rs_r.at[d],
            device_id=s_peer(d), device_id_type=MESH))
    for c in sq_copies:
        c.start()
    for d in range(1, RING):
        to = (sec + d) % RING
        part[to] = acc[pl.ds(to * own, own), :].astype(jnp.bfloat16)
        rs_copies[d - 1].start()

    row8 = lax.broadcasted_iota(jnp.int32, (own, 8), 0)
    lane6 = lax.broadcasted_iota(jnp.int32, (own, 6), 1)
    row6 = lax.broadcasted_iota(jnp.int32, (own, 6), 0)
    row1 = row8[:, :1]
    place = jnp.zeros((own, 1), jnp.int32)
    length = jnp.zeros((own, 1), jnp.int32)
    limit = jnp.zeros((own, 1), jnp.int32)
    token6 = jnp.zeros((own, 6), jnp.int32)
    for r in range(8):
        inside = (row1 >= 6 * r) & (row1 < 6 * r + 6)
        place = jnp.where(inside, row1 - 6 * r, place)
        length = jnp.where(inside, length_ref[r], length)
        limit = jnp.where(inside, accepted_ref[r], limit)
        token6 = jnp.where(row6 == lane6 + 6 * r, jnp.broadcast_to(tok_ref[pl.ds(r, 1), :], (own, 6)), token6)
    token = jnp.sum(token6.astype(jnp.float32), axis=1, keepdims=True).astype(jnp.int32)
    unit = lax.broadcasted_iota(jnp.int32, (own, HD), 1)
    half = jnp.where(unit >= HD // 2, unit - HD // 2, unit).astype(jnp.float32)
    frequency = jnp.exp(half * jnp.float32(-2.0 / HD * 13.122363377404328))
    angle = (length + place).astype(jnp.float32) * frequency
    cosine = jnp.cos(angle)
    sine = jnp.where(unit < HD // 2, -jnp.sin(angle), jnp.sin(angle))

    for c in sq_copies:
        c.wait_recv()
    squares = jnp.sum(jnp.sum(sq_in[...], axis=0), axis=0, keepdims=True)
    scale_row = lax.rsqrt(squares / D + 1e-05)
    lane = lax.broadcasted_iota(jnp.int32, (own, rows), 1)
    sub = lax.broadcasted_iota(jnp.int32, (own, rows), 0)
    scale = jnp.sum(jnp.where(lane == sub + sec * own, scale_row, 0.0), axis=1, keepdims=True)

    total = acc[pl.ds(sec * own, own), :]
    for d in range(1, RING):
        rs_copies[d - 1].wait_recv()
        total = total + landed[(sec + RING - d) % RING].astype(jnp.float32)
    full = jnp.where(scale == 0.0, 0.0, total * scale)
    logits = full[:, :vocab]
    query = full[:, vocab:]
    ids = lax.broadcasted_iota(jnp.int32, (own, vocab), 1) + tgt * vocab
    picked = jnp.sum(jnp.where(ids == token, logits, 0.0), axis=1, keepdims=True)
    exps = jnp.sum(jnp.exp(logits), axis=1, keepdims=True)
    eye = lax.broadcasted_iota(jnp.int32, (own, 128), 0) == lax.broadcasted_iota(jnp.int32, (own, 128), 1)
    exp_row = jnp.sum(jnp.where(eye, exps, 0.0), axis=0, keepdims=True)
    pick_row = jnp.sum(jnp.where(eye, picked, 0.0), axis=0, keepdims=True)
    which = lax.broadcasted_iota(jnp.int32, (8, 128), 0)
    msg1[...] = jnp.where(which == 0, exp_row, jnp.where(which == 1, pick_row, 0.0))

    def exchange(msg, inbox, at, peer, ssem, rsem):
        copies = [pltpu.make_async_remote_copy(
            msg, inbox.at[at], ssem.at[d], rsem.at[d], device_id=peer(d), device_id_type=MESH)
            for d in range(1, RING)]
        for c in copies:
            c.start()
        inbox[at] = msg[...]
        return copies

    e1 = exchange(msg1, in1, z, z_peer, e1s, e1r)
    rotated = query * cosine + pltpu.roll(query, HD // 2, 1) * sine
    dq_ref[...] = jnp.where(place < limit, rotated, 0.0).astype(jnp.bfloat16)
    for c in e1:
        c.wait_recv()
    msg2[...] = jnp.sum(in1[...], axis=0)
    e2 = exchange(msg2, in2, y, y_peer, e2s, e2r)
    for c in e2:
        c.wait_recv()
    sums = jnp.sum(in2[...], axis=0)
    lp_row = sums[1:2] - jnp.log(sums[0:1])
    sub8 = lax.broadcasted_iota(jnp.int32, (8, 128), 0)
    lane8 = lax.broadcasted_iota(jnp.int32, (8, 128), 1)
    out_lane = lax.broadcasted_iota(jnp.int32, (8, 6), 1)
    out = jnp.zeros((8, 6), jnp.float32)
    for p in range(6):
        col = jnp.sum(jnp.where(lane8 == 6 * sub8 + p, lp_row, 0.0), axis=1, keepdims=True)
        out = jnp.where(out_lane == p, col, out)
    lp_ref[...] = out

    for c in first + sum(second, []) + sq_copies + rs_copies + e1 + e2:
        c.wait_send()


def local(
    hidden, norm_gain, vocab_weight, draft_gain, query_weight, draft_tokens, accepted, cache_lengths
):
    rows, vocab = hidden.shape[0], vocab_weight.shape[1]
    wide = vocab + HD
    depth = vocab_weight.shape[0]
    own = rows // RING
    any_spec = pl.BlockSpec(memory_space=pl.ANY)
    vmem, smem = pl.BlockSpec(memory_space=pltpu.VMEM), pl.BlockSpec(memory_space=pltpu.SMEM)
    bf16, f32 = jnp.bfloat16, jnp.float32
    dma = pltpu.SemaphoreType.DMA
    lp, dq = pl.pallas_call(
        kernel,
        out_shape=(
            jax.ShapeDtypeStruct(draft_tokens.shape, f32),
            jax.ShapeDtypeStruct((own, HD), bf16),
        ),
        in_specs=[any_spec] * 5 + [vmem, smem, smem],
        out_specs=(vmem, vmem),
        scratch_shapes=[
            pltpu.VMEM((8, 8, 16, rows), bf16),
            pltpu.VMEM((8, 8, 16, rows), bf16),
            pltpu.VMEM((depth, wide), bf16),
            pltpu.VMEM((8, 8, 16, wide), bf16),
            pltpu.VMEM((8, 8, 16, wide), bf16),
            pltpu.VMEM((rows, wide), f32),
            pltpu.VMEM((8, own, wide), bf16),
            pltpu.VMEM((8, own, wide), bf16),
            pltpu.VMEM((8, rows), f32),
            pltpu.VMEM((8, 8, rows), f32),
            pltpu.VMEM((2, 16, 128), bf16),
            pltpu.VMEM((8, 128), f32),
            pltpu.VMEM((8, 128), f32),
            pltpu.VMEM((8, 8, 128), f32),
            pltpu.VMEM((8, 8, 128), f32),
            dma((6,)),
            dma((2, 8)), dma((2, 8)),
            dma((2, 2, 4)), dma((2, 2, 4)),
            dma((8,)), dma((8,)),
            dma((8,)), dma((8,)),
            dma((8,)), dma((8,)),
            dma((8,)), dma((8,)),
        ],
        compiler_params=pltpu.CompilerParams(
            collective_id=0, has_side_effects=True, vmem_limit_bytes=40 * 1024 * 1024
        ),
    )(
        hidden.T,
        norm_gain.reshape(16, 128),
        vocab_weight,
        draft_gain.reshape(128, 128),
        query_weight,
        draft_tokens,
        accepted,
        cache_lengths,
    )
    return lp, dq


def solution(mesh):
    return jax.shard_map(
        local,
        mesh=mesh,
        in_specs=(
            P(None, ("sec", "tgt")),
            P("sec"),
            P("sec", "tgt"),
            P(),
            P("sec", "tgt"),
            P("sec", None),
            P("sec"),
            P("sec"),
        ),
        out_specs=(P("sec", None), P("sec", "tgt")),
        check_vma=False,
    )
```

time: 344 us -> 67.3 us (0.20)
  the two profiles are of different devices: /device:TPU:2 before, /device:TPU:1 now
where the time goes in v1:
time: 67.3 us; the launch traced here: 66.9 us
  Pallas kernels  57.6 us (86%)
  local copies, waits for them, and re-layouts  8.59 us (13%)
    pallas_call x1, Pallas kernels, local(): pl.pallas_call(kernel, out_shape=(jax.ShapeDtypeStruct(draft_tokens.shape...  57.6 us
    unnamed x18, local copies, waits for them, and re-layouts  8.59 us

profile of v1, /device:TPU:1, one launch (start us, length us, event | category | flops | bytes accessed | tf_op | source)
XLA Modules:
  0.0 66.9 jit_solution(10442625917121486846)
XLA Ops:
  0.6 0.0 copy-start
  0.6 2.2 %copy-done = bf16[2048,1024]{1,0:T(8,128)(2,1)S(1)} copy-done((bf16[2048,1024]{1,0:T(8,128)(2,1)S(1)}, bf16[2048,1024]{1,0:T(8,128)(2,1)}, u32[]{:S(2)}) %copy-start) | copy-done | bytes 4194328
  2.8 0.0 copy-start.1
  2.8 1.0 %copy-done.1 = bf16[2048,128]{1,0:T(8,128)(2,1)S(1)} copy-done((bf16[2048,128]{1,0:T(8,128)(2,1)S(1)}, bf16[2048,128]{1,0:T(8,128)(2,1)}, u32[]{:S(2)}) %copy-start.1) | copy-done | bytes 524312
  3.9 0.0 copy-start.2
  3.9 0.8 %copy-done.2 = bf16[16384]{0:T(1024)(128)(2,1)S(1)} copy-done((bf16[16384]{0:T(1024)(128)(2,1)S(1)}, bf16[16384]{0:T(1024)(128)(2,1)}, u32[]{:S(2)}) %copy-start.2) | copy-done | bytes 32792
  4.6 0.0 copy-start.3
  4.6 0.7 %copy-done.3 = bf16[384,32]{0,1:T(8,128)(2,1)S(1)} copy-done((bf16[384,32]{0,1:T(8,128)(2,1)S(1)}, bf16[384,32]{0,1:T(8,128)(2,1)}, u32[]{:S(2)}) %copy-start.3) | copy-done | bytes 24600
  5.4 0.0 copy-start.4
  5.4 0.7 %copy-done.4 = bf16[2048]{0:T(1024)(128)(2,1)S(1)} copy-done((bf16[2048]{0:T(1024)(128)(2,1)S(1)}, bf16[2048]{0:T(1024)(128)(2,1)}, u32[]{:S(2)}) %copy-start.4) | copy-done | bytes 4120
  6.0 0.0 copy-start.5
  6.0 0.7 %copy-done.5 = s32[8,6]{1,0:T(8,128)S(1)} copy-done((s32[8,6]{1,0:T(8,128)S(1)}, s32[8,6]{1,0:T(8,128)}, u32[]{:S(2)}) %copy-start.5) | copy-done | bytes 216
  6.7 0.0 copy-start.6
  6.7 0.7 copy-done.6
  7.4 0.0 copy-start.7
  7.4 0.7 copy-done.7
  8.0 57.6 %shard_map.95 = (f32[8,6]{1,0:T(8,128)S(1)}, bf16[48,128]{1,0:T(8,128)(2,1)S(1)}) custom-call(bf16[32,384]{1,0:T(8,128)(2,1)S(1)} %bitcast.4, bf16[16,128]{1,0:T(8,128)(2,1)S(1)} %bitcast.5, bf16[2048,1024]{1,0:T(8,128)(2,1)S(1)} %copy-done, bf16[128,128]{1,0:T(8,128)(2,1)S(1)} %bitcast.3, bf16[2048,128]{1,0:T(8,128)(2,1)S(1)} %copy-done.1, ...), custom_call_target="tpu_custom_call" | custom-call | tf_op jit(solution)/shard_map/pallas_call | solution.py:235
  65.7 0.6 copy.12
  66.3 0.6 copy.13
Async XLA Ops:
  0.6 2.2 %copy-start = (bf16[2048,1024]{1,0:T(8,128)(2,1)S(1)}, bf16[2048,1024]{1,0:T(8,128)(2,1)}, u32[]{:S(2)}) copy-start(bf16[2048,1024]{1,0:T(8,128)(2,1)} %w_hbm.1) | copy-start | bytes 12582916
  2.8 1.0 %copy-start.1 = (bf16[2048,128]{1,0:T(8,128)(2,1)S(1)}, bf16[2048,128]{1,0:T(8,128)(2,1)}, u32[]{:S(2)}) copy-start(bf16[2048,128]{1,0:T(8,128)(2,1)} %wq_hbm.1) | copy-start | bytes 1572868
  3.9 0.8 %copy-start.2 = (bf16[16384]{0:T(1024)(128)(2,1)S(1)}, bf16[16384]{0:T(1024)(128)(2,1)}, u32[]{:S(2)}) copy-start(bf16[16384]{0:T(1024)(128)(2,1)} %param.11) | copy-start | bytes 98308
  4.6 0.7 %copy-start.3 = (bf16[384,32]{0,1:T(8,128)(2,1)S(1)}, bf16[384,32]{0,1:T(8,128)(2,1)}, u32[]{:S(2)}) copy-start(bf16[384,32]{0,1:T(8,128)(2,1)} %param.8) | copy-start | bytes 73732
  5.4 0.7 %copy-start.4 = (bf16[2048]{0:T(1024)(128)(2,1)S(1)}, bf16[2048]{0:T(1024)(128)(2,1)}, u32[]{:S(2)}) copy-start(bf16[2048]{0:T(1024)(128)(2,1)} %param.9) | copy-start | bytes 12292
  6.0 0.7 %copy-start.5 = (s32[8,6]{1,0:T(8,128)S(1)}, s32[8,6]{1,0:T(8,128)}, u32[]{:S(2)}) copy-start(s32[8,6]{1,0:T(8,128)} %tok_ref.1) | copy-start | bytes 580
  6.7 0.7 copy-start.6
  7.4 0.7 copy-start.7

commit v2 on v1

--- a/solution.py
+++ b/solution.py
@@ -9,12 +9,14 @@
 HD = 128
 RING = 8
 MESH = pl.DeviceIdType.MESH
+SLOT = (0, 1, 3, 5, 7, 6, 4, 2)
+PARTS = ((0, 3, 2), (3, 5, 2))
 
 
 def kernel(
     h_hbm, gain_hbm, w_hbm, dgain_hbm, wq_hbm, tok_ref, accepted_ref, length_ref,
     lp_ref, dq_ref,
-    ga, gb, raw, wa, wb, acc, part, landed, sq, sq_in, gains, msg1, msg2, in1, in2,
+    ga, gb, raw, wa, wb, acc, mine, part, landed, sq, sq_pair, sq_in, gains, msg1, msg2, in1, in2,
     local_sem, p1s, p1r, p2s, p2r, rs_s, rs_r, sq_s, sq_r, e1s, e1r, e2s, e2r,
 ):
     tgt = lax.axis_index("tgt")
@@ -29,8 +31,18 @@
     def y_peer(d):
         return (((y + d) % RING) * RING + z, sec)
 
-    def s_peer(d):
-        return (tgt, (sec + d) % RING)
+    x, core = sec // 2, sec % 2
+    sibling = (tgt, 2 * x + 1 - core)
+
+    def x_peer(d):
+        return (tgt, 2 * ((x + d) % 4) + core)
+
+    barrier = pltpu.get_barrier_semaphore()
+    for d in (4, 3, 5, 2, 6, 1, 7):
+        for peer in (z_peer(d), y_peer(d)):
+            pl.semaphore_signal(barrier, inc=1, device_id=peer, device_id_type=MESH)
+    for peer in (sibling, x_peer(1), x_peer(2), x_peer(3)):
+        pl.semaphore_signal(barrier, inc=1, device_id=peer, device_id_type=MESH)
 
     w_copies = [
         pltpu.make_async_copy(w_hbm, raw.at[:, pl.ds(0, vocab)], local_sem.at[0]),
@@ -39,53 +51,82 @@
         pltpu.make_async_copy(dgain_hbm.at[pl.ds(sec * 16, 16)], gains.at[1], local_sem.at[3]),
     ]
     h_copies = [
-        pltpu.make_async_copy(h_hbm.at[pl.ds(0, 16)], ga.at[y, z], local_sem.at[4]),
-        pltpu.make_async_copy(h_hbm.at[pl.ds(16, 16)], gb.at[z, y], local_sem.at[5]),
+        pltpu.make_async_copy(h_hbm.at[pl.ds(0, 16)], ga.at[y, 0], local_sem.at[4]),
+        pltpu.make_async_copy(h_hbm.at[pl.ds(16, 16)], gb.at[z, 0], local_sem.at[5]),
     ]
     for c in h_copies + w_copies:
         c.start()
 
-    barrier = pltpu.get_barrier_semaphore()
-    for d in range(1, RING):
-        for peer in (z_peer(d), y_peer(d), s_peer(d)):
-            pl.semaphore_signal(barrier, inc=1, device_id=peer, device_id_type=MESH)
-    pl.semaphore_wait(barrier, 3 * (RING - 1))
-
-    first = []
-    for d in range(1, RING):
-        first.append(pltpu.make_async_remote_copy(
-            h_hbm.at[pl.ds(0, 16)], ga.at[y, z], p1s.at[0, d], p1r.at[0, d],
-            device_id=z_peer(d), device_id_type=MESH))
-        first.append(pltpu.make_async_remote_copy(
-            h_hbm.at[pl.ds(16, 16)], gb.at[z, y], p1s.at[1, d], p1r.at[1, d],
-            device_id=y_peer(d), device_id_type=MESH))
-    for c in first:
-        c.start()
+    pl.semaphore_wait(barrier, 2 * (RING - 1) + 4)
+
+    def first_copies(d):
+        to = SLOT[RING - d]
+        return [
+            pltpu.make_async_remote_copy(
+                h_hbm.at[pl.ds(0, 16)], ga.at[y, to], p1s.at[0, d], p1r.at[0, d],
+                device_id=z_peer(d), device_id_type=MESH),
+            pltpu.make_async_remote_copy(
+                h_hbm.at[pl.ds(16, 16)], gb.at[z, to], p1s.at[1, d], p1r.at[1, d],
+                device_id=y_peer(d), device_id_type=MESH),
+        ]
+
+    first = {d: first_copies(d) for d in range(1, RING)}
+    for d in (1, 7, 2, 6, 3, 5, 4):
+        for c in first[d]:
+            c.start()
+
+    def ring_copies(p):
+        at_slot, count, up = PARTS[p]
+        near, far, third, fourth = [], [], [], []
+        for k, (buf, at, peer) in enumerate(((ga, y, y_peer), (gb, z, z_peer))):
+            for way in (0, 1):
+                step = 1 if way == 0 else RING - 1
+                from2 = (at + 2 * (RING - step)) % RING
+                lo, n = (at_slot, up) if way == 0 else (at_slot + up, count - up)
+                for kind, (group, ref, hops) in enumerate((
+                    (near, buf.at[at, pl.ds(at_slot, count)], step),
+                    (far, buf.at[at, pl.ds(at_slot, count)], 2 * step),
+                    (third, buf.at[from2, pl.ds(at_slot, count)], step),
+                    (fourth, buf.at[from2, pl.ds(lo, n)] if n else None, 2 * step),
+                )):
+                    if ref is not None:
+                        group.append(pltpu.make_async_remote_copy(
+                            ref, ref, p2s.at[p, k, way, kind], p2r.at[p, k, way, kind],
+                            device_id=peer(hops), device_id_type=MESH))
+        return near, far, third, fourth
+
+    second = [ring_copies(p) for p in range(len(PARTS))]
+
+    def spread(p):
+        for slot in range(PARTS[p][0], PARTS[p][0] + PARTS[p][1]):
+            if slot > 0:
+                for c in first[RING - SLOT.index(slot)]:
+                    c.wait_recv()
+        for c in second[p][1] + second[p][0]:
+            c.start()
+
+    def pass_on(p):
+        for c in second[p][1]:
+            c.wait_recv()
+        for c in second[p][3] + second[p][2]:
+            c.start()
+
+    def arrived(kind):
+        for group in second:
+            for c in group[kind]:
+                c.wait_recv()
+
     for c in h_copies:
         c.wait()
-    for c in first:
-        c.wait_recv()
-
-    def ring_copies(s):
-        out = []
-        for k, (buf, at, peer) in enumerate(((ga, y, y_peer), (gb, z, z_peer))):
-            for way in (0, 1):
-                step = 1 if way == 0 else -1
-                block = (at - step * (s - 1)) % RING if s > 1 else at
-                ref = buf.at[block]
-                if s == 4:
-                    ref = buf.at[block, pl.ds(4 * way, 4)]
-                out.append(pltpu.make_async_remote_copy(
-                    ref, ref, p2s.at[k, way, s - 1], p2r.at[k, way, s - 1],
-                    device_id=peer(step), device_id_type=MESH))
-        return out
-
-    second = [ring_copies(s) for s in range(1, 5)]
-    for c in second[0]:
-        c.start()
+    for p in range(len(PARTS)):
+        spread(p)
 
     for c in w_copies:
         c.wait()
+
+    def slot_of(rel):
+        return jnp.where(rel == 0, 0, jnp.where(rel <= 4, 2 * rel - 1, 16 - 2 * rel))
+
     gt = jnp.transpose(gains[0].astype(jnp.float32))
     dgt = jnp.transpose(gains[1].astype(jnp.float32))
     for j in range(16):
@@ -95,8 +136,8 @@
         for i in range(4):
             yy, zz = j // 2, 4 * (j % 2) + i
             for wide, values in ((pl.ds(0, vocab), left), (pl.ds(vocab, HD), right)):
-                wa[yy, zz, :, wide] = values[32 * i:32 * i + 16]
-                wb[zz, yy, :, wide] = values[32 * i + 16:32 * i + 32]
+                wa[yy, slot_of((zz + RING - z) % RING), :, wide] = values[32 * i:32 * i + 16]
+                wb[zz, slot_of((yy + RING - y) % RING), :, wide] = values[32 * i + 16:32 * i + 32]
 
     def take(h_parts, w_parts, fresh):
         h = jnp.concatenate([v.reshape(128, rows) for v in h_parts], axis=0)
@@ -114,33 +155,56 @@
                 acc[:, cols] += prod
 
     take([ga[y], gb[z]], [(wa, y), (wb, z)], True)
-    for s in range(1, 4):
-        for c in second[s - 1]:
-            c.wait_recv()
-        for c in second[s]:
-            c.start()
+    def take_pair(s):
         for buf, w, at in ((ga, wa, y), (gb, wb, z)):
             b1, b2 = (at + s) % RING, (at + RING - s) % RING
             take([buf[b1], buf[b2]], [(w, b1), (w, b2)], False)
-    for c in second[3]:
-        c.wait_recv()
+
+    for p in range(len(PARTS)):
+        pass_on(p)
+    arrived(0)
+    take_pair(1)
+    take_pair(2)
+    arrived(2)
+    take_pair(3)
+    arrived(3)
     far_y, far_z = (y + 4) % RING, (z + 4) % RING
     take([ga[far_y], gb[far_z]], [(wa, far_y), (wb, far_z)], False)
 
-    sq_copies, rs_copies = [], []
-    sq_in[sec] = sq[...]
-    for d in range(1, RING):
-        sq_copies.append(pltpu.make_async_remote_copy(
-            sq, sq_in.at[sec], sq_s.at[d], sq_r.at[d], device_id=s_peer(d), device_id_type=MESH))
-        rs_copies.append(pltpu.make_async_remote_copy(
-            part.at[(sec + d) % RING], landed.at[sec], rs_s.at[d], rs_r.at[d],
-            device_id=s_peer(d), device_id_type=MESH))
-    for c in sq_copies:
+    order = (2, 1, 3, 0)
+    pair_sq = pltpu.make_async_remote_copy(
+        sq, sq_in.at[0], sq_s.at[0], sq_r.at[0], device_id=sibling, device_id_type=MESH)
+    pair_sq.start()
+    pair_copies, x_copies, x_sq = [], [], []
+    for i, d in enumerate(order):
+        pair_copies.append(pltpu.make_async_remote_copy(
+            part.at[i], landed.at[i], rs_s.at[i], rs_r.at[i], device_id=sibling, device_id_type=MESH))
+        if d:
+            x_copies.append(pltpu.make_async_remote_copy(
+                part.at[4 + i], landed.at[4 + i], rs_s.at[4 + i], rs_r.at[4 + i],
+                device_id=x_peer(d), device_id_type=MESH))
+            x_sq.append(pltpu.make_async_remote_copy(
+                sq_pair, sq_in.at[d], sq_s.at[d], sq_r.at[d],
+                device_id=x_peer(d), device_id_type=MESH))
+
+    def rows_of(d, side):
+        return pl.ds((2 * ((x + d) % 4) + side) * own, own)
+
+    for i, d in enumerate(order):
+        part[i] = acc[rows_of(d, 1 - core), :].astype(jnp.bfloat16)
+        pair_copies[i].start()
+    pair_sq.wait_recv()
+    sq_pair[...] = sq[...] + sq_in[0]
+    for c in x_sq:
         c.start()
-    for d in range(1, RING):
-        to = (sec + d) % RING
-        part[to] = acc[pl.ds(to * own, own), :].astype(jnp.bfloat16)
-        rs_copies[d - 1].start()
+    for i, d in enumerate(order):
+        pair_copies[i].wait_recv()
+        both = acc[rows_of(d, core), :] + landed[i].astype(jnp.float32)
+        if d:
+            part[4 + i] = both.astype(jnp.bfloat16)
+            x_copies[i].start()
+        else:
+            mine[...] = both
 
     row8 = lax.broadcasted_iota(jnp.int32, (own, 8), 0)
     lane6 = lax.broadcasted_iota(jnp.int32, (own, 6), 1)
@@ -164,18 +228,19 @@
     cosine = jnp.cos(angle)
     sine = jnp.where(unit < HD // 2, -jnp.sin(angle), jnp.sin(angle))
 
-    for c in sq_copies:
+    for c in x_sq:
         c.wait_recv()
-    squares = jnp.sum(jnp.sum(sq_in[...], axis=0), axis=0, keepdims=True)
+    squares = sq_pair[...] + sq_in[1] + sq_in[2] + sq_in[3]
+    squares = jnp.sum(squares, axis=0, keepdims=True)
     scale_row = lax.rsqrt(squares / D + 1e-05)
     lane = lax.broadcasted_iota(jnp.int32, (own, rows), 1)
     sub = lax.broadcasted_iota(jnp.int32, (own, rows), 0)
     scale = jnp.sum(jnp.where(lane == sub + sec * own, scale_row, 0.0), axis=1, keepdims=True)
 
-    total = acc[pl.ds(sec * own, own), :]
-    for d in range(1, RING):
-        rs_copies[d - 1].wait_recv()
-        total = total + landed[(sec + RING - d) % RING].astype(jnp.float32)
+    total = mine[...]
+    for i in range(3):
+        x_copies[i].wait_recv()
+        total = total + landed[4 + i].astype(jnp.float32)
     full = jnp.where(scale == 0.0, 0.0, total * scale)
     logits = full[:, :vocab]
     query = full[:, vocab:]
@@ -217,7 +282,7 @@
         out = jnp.where(out_lane == p, col, out)
     lp_ref[...] = out
 
-    for c in first + sum(second, []) + sq_copies + rs_copies + e1 + e2:
+    for c in sum(first.values(), []) + sum([sum(g, []) for g in second], []) + [pair_sq] + x_sq + pair_copies + x_copies + e1 + e2:
         c.wait_send()
 
 
@@ -247,10 +312,12 @@
             pltpu.VMEM((8, 8, 16, wide), bf16),
             pltpu.VMEM((8, 8, 16, wide), bf16),
             pltpu.VMEM((rows, wide), f32),
+            pltpu.VMEM((own, wide), f32),
             pltpu.VMEM((8, own, wide), bf16),
             pltpu.VMEM((8, own, wide), bf16),
             pltpu.VMEM((8, rows), f32),
-            pltpu.VMEM((8, 8, rows), f32),
+            pltpu.VMEM((8, rows), f32),
+            pltpu.VMEM((4, 8, rows), f32),
             pltpu.VMEM((2, 16, 128), bf16),
             pltpu.VMEM((8, 128), f32),
             pltpu.VMEM((8, 128), f32),
@@ -258,14 +325,14 @@
             pltpu.VMEM((8, 8, 128), f32),
             dma((6,)),
             dma((2, 8)), dma((2, 8)),
-            dma((2, 2, 4)), dma((2, 2, 4)),
+            dma((len(PARTS), 2, 2, 4)), dma((len(PARTS), 2, 2, 4)),
             dma((8,)), dma((8,)),
             dma((8,)), dma((8,)),
             dma((8,)), dma((8,)),
             dma((8,)), dma((8,)),
         ],
         compiler_params=pltpu.CompilerParams(
-            collective_id=0, has_side_effects=True, vmem_limit_bytes=40 * 1024 * 1024
+            collective_id=0, has_side_effects=True, vmem_limit_bytes=60 * 1024 * 1024
         ),
     )(
         hidden.T,

time: 67.3 us -> 56.2 us (0.84)
  local copies, waits for them, and re-layouts: 8.59 us -> 2.57 us
  Pallas kernels: 57.6 us -> 52.4 us
    unnamed x18 -> x2, local copies, waits for them, and re-layouts: 8.59 us -> 2.57 us
    pallas_call x1, Pallas kernels: 57.6 us -> 52.4 us  [local(): pl.pallas_call(kernel, out_shape=(jax.ShapeDtypeStruct(draft_tokens.shape...]
where the time goes in v2:
time: 56.2 us; the launch traced here: 55.6 us
  Pallas kernels  52.4 us (93%)
  local copies, waits for them, and re-layouts  2.57 us (5%)
  between operations  0.64 us (1%)
    pallas_call x1, Pallas kernels, local(): pl.pallas_call(kernel, out_shape=(jax.ShapeDtypeStruct(draft_tokens.shape...  52.4 us
    unnamed x2, local copies, waits for them, and re-layouts  2.57 us

profile of v2, /device:TPU:1, one launch (start us, length us, event | category | flops | bytes accessed | tf_op | source)
XLA Modules:
  0.0 55.6 jit_solution(8065388389628390428)
XLA Ops:
  0.6 52.4 %shard_map.95 = (f32[8,6]{1,0:T(8,128)}, bf16[48,128]{1,0:T(8,128)(2,1)}) custom-call(bf16[32,384]{1,0:T(8,128)(2,1)} %bitcast.4, bf16[16,128]{1,0:T(8,128)(2,1)} %bitcast.5, bf16[2048,1024]{1,0:T(8,128)(2,1)} %w_hbm.1, bf16[128,128]{1,0:T(8,128)(2,1)} %bitcast.3, bf16[2048,128]{1,0:T(8,128)(2,1)} %wq_hbm.1, s32[8,6]{1,0:T(8,128)} %tok_ref.1, ...), custom_call_target="tpu_custom_call" | custom-call | tf_op jit(solution)/shard_map/pallas_call | solution.py:300
  53.1 1.3 %copy.12 = f32[8,6]{1,0:T(8,128)} copy(f32[8,6]{1,0:T(8,128)} %get-tuple-element.4) | data formatting | bytes 384
  54.3 1.3 %copy.13 = bf16[48,128]{1,0:T(8,128)(2,1)} copy(bf16[48,128]{1,0:T(8,128)(2,1)} %get-tuple-element.5) | data formatting | bytes 24576

commit v3 on v2

--- a/solution.py
+++ b/solution.py
@@ -16,7 +16,7 @@
 def kernel(
     h_hbm, gain_hbm, w_hbm, dgain_hbm, wq_hbm, tok_ref, accepted_ref, length_ref,
     lp_ref, dq_ref,
-    ga, gb, raw, wa, wb, acc, mine, part, landed, sq, sq_pair, sq_in, gains, msg1, msg2, in1, in2,
+    ga, gb, raw, wa, wb, acc, mine, part, landed, sq, sq_own, sq_pair, sq_in, gains, msg1, msg2, in1, in2,
     local_sem, p1s, p1r, p2s, p2r, rs_s, rs_r, sq_s, sq_r, e1s, e1r, e2s, e2r,
 ):
     tgt = lax.axis_index("tgt")
@@ -172,8 +172,9 @@
     take([ga[far_y], gb[far_z]], [(wa, far_y), (wb, far_z)], False)
 
     order = (2, 1, 3, 0)
+    sq_own[...] = jnp.sum(sq[...], axis=0, keepdims=True)
     pair_sq = pltpu.make_async_remote_copy(
-        sq, sq_in.at[0], sq_s.at[0], sq_r.at[0], device_id=sibling, device_id_type=MESH)
+        sq_own, sq_in.at[0], sq_s.at[0], sq_r.at[0], device_id=sibling, device_id_type=MESH)
     pair_sq.start()
     pair_copies, x_copies, x_sq = [], [], []
     for i, d in enumerate(order):
@@ -194,7 +195,7 @@
         part[i] = acc[rows_of(d, 1 - core), :].astype(jnp.bfloat16)
         pair_copies[i].start()
     pair_sq.wait_recv()
-    sq_pair[...] = sq[...] + sq_in[0]
+    sq_pair[...] = sq_own[...] + sq_in[0]
     for c in x_sq:
         c.start()
     for i, d in enumerate(order):
@@ -231,7 +232,6 @@
     for c in x_sq:
         c.wait_recv()
     squares = sq_pair[...] + sq_in[1] + sq_in[2] + sq_in[3]
-    squares = jnp.sum(squares, axis=0, keepdims=True)
     scale_row = lax.rsqrt(squares / D + 1e-05)
     lane = lax.broadcasted_iota(jnp.int32, (own, rows), 1)
     sub = lax.broadcasted_iota(jnp.int32, (own, rows), 0)
@@ -250,8 +250,8 @@
     eye = lax.broadcasted_iota(jnp.int32, (own, 128), 0) == lax.broadcasted_iota(jnp.int32, (own, 128), 1)
     exp_row = jnp.sum(jnp.where(eye, exps, 0.0), axis=0, keepdims=True)
     pick_row = jnp.sum(jnp.where(eye, picked, 0.0), axis=0, keepdims=True)
-    which = lax.broadcasted_iota(jnp.int32, (8, 128), 0)
-    msg1[...] = jnp.where(which == 0, exp_row, jnp.where(which == 1, pick_row, 0.0))
+    msg1[0:1] = exp_row
+    msg1[1:2] = pick_row
 
     def exchange(msg, inbox, at, peer, ssem, rsem):
         copies = [pltpu.make_async_remote_copy(
@@ -300,8 +300,8 @@
     lp, dq = pl.pallas_call(
         kernel,
         out_shape=(
-            jax.ShapeDtypeStruct(draft_tokens.shape, f32),
-            jax.ShapeDtypeStruct((own, HD), bf16),
+            pltpu.VMEM(draft_tokens.shape, f32),
+            pltpu.VMEM((own, HD), bf16),
         ),
         in_specs=[any_spec] * 5 + [vmem, smem, smem],
         out_specs=(vmem, vmem),
@@ -316,13 +316,14 @@
             pltpu.VMEM((8, own, wide), bf16),
             pltpu.VMEM((8, own, wide), bf16),
             pltpu.VMEM((8, rows), f32),
-            pltpu.VMEM((8, rows), f32),
-            pltpu.VMEM((4, 8, rows), f32),
+            pltpu.VMEM((1, rows), f32),
+            pltpu.VMEM((1, rows), f32),
+            pltpu.VMEM((4, 1, rows), f32),
             pltpu.VMEM((2, 16, 128), bf16),
-            pltpu.VMEM((8, 128), f32),
-            pltpu.VMEM((8, 128), f32),
-            pltpu.VMEM((8, 8, 128), f32),
-            pltpu.VMEM((8, 8, 128), f32),
+            pltpu.VMEM((2, 128), f32),
+            pltpu.VMEM((2, 128), f32),
+            pltpu.VMEM((8, 2, 128), f32),
+            pltpu.VMEM((8, 2, 128), f32),
             dma((6,)),
             dma((2, 8)), dma((2, 8)),
             dma((len(PARTS), 2, 2, 4)), dma((len(PARTS), 2, 2, 4)),

time: 56.2 us -> 53.4 us (0.950)
  local copies, waits for them, and re-layouts: 2.57 us -> 1.19 us
  Pallas kernels: 52.4 us -> 51.1 us
    unnamed x2, local copies, waits for them, and re-layouts: 2.57 us -> 1.19 us
    pallas_call x1, Pallas kernels: 52.4 us -> 51.1 us  [local(): pl.pallas_call(kernel, out_shape=(pltpu.VMEM(draft_tokens.shape, f32), pl...]
where the time goes in v3:
time: 53.4 us; the launch traced here: 53 us
  Pallas kernels  51.1 us (96%)
  local copies, waits for them, and re-layouts  1.19 us (2%)
  between operations  0.64 us (1%)
    pallas_call x1, Pallas kernels, local(): pl.pallas_call(kernel, out_shape=(pltpu.VMEM(draft_tokens.shape, f32), pl...  51.1 us
    unnamed x2, local copies, waits for them, and re-layouts  1.19 us

profile of v3, /device:TPU:1, one launch (start us, length us, event | category | flops | bytes accessed | tf_op | source)
XLA Modules:
  0.0 53.0 jit_solution(10738649806154470964)
XLA Ops:
  0.6 51.1 %shard_map.95 = (f32[8,6]{1,0:T(8,128)S(1)}, bf16[48,128]{1,0:T(8,128)(2,1)S(1)}) custom-call(bf16[32,384]{1,0:T(8,128)(2,1)} %bitcast.4, bf16[16,128]{1,0:T(8,128)(2,1)} %bitcast.5, bf16[2048,1024]{1,0:T(8,128)(2,1)} %w_hbm.1, bf16[128,128]{1,0:T(8,128)(2,1)} %bitcast.3, bf16[2048,128]{1,0:T(8,128)(2,1)} %wq_hbm.1, s32[8,6]{1,0:T(8,128)} %tok_ref.1, ...), custom_call_target="tpu_custom_call" | custom-call | tf_op jit(solution)/shard_map/pallas_call | solution.py:300
  51.8 0.6 %copy.12 = f32[8,6]{1,0:T(8,128)} copy(f32[8,6]{1,0:T(8,128)S(1)} %get-tuple-element.2) | data formatting | bytes 384
  52.4 0.6 %copy.13 = bf16[48,128]{1,0:T(8,128)(2,1)} copy(bf16[48,128]{1,0:T(8,128)(2,1)S(1)} %get-tuple-element.3) | data formatting | bytes 24576

commit v4 on v3

--- a/solution.py
+++ b/solution.py
@@ -98,18 +98,20 @@
     second = [ring_copies(p) for p in range(len(PARTS))]
 
     def spread(p):
-        for slot in range(PARTS[p][0], PARTS[p][0] + PARTS[p][1]):
-            if slot > 0:
-                for c in first[RING - SLOT.index(slot)]:
-                    c.wait_recv()
-        for c in second[p][1] + second[p][0]:
-            c.start()
+        near, far = second[p][:2]
+        for k in (0, 1):
+            for slot in range(PARTS[p][0], PARTS[p][0] + PARTS[p][1]):
+                if slot > 0:
+                    first[RING - SLOT.index(slot)][k].wait_recv()
+            for c in far[2 * k:2 * k + 2] + near[2 * k:2 * k + 2]:
+                c.start()
 
     def pass_on(p):
-        for c in second[p][1]:
-            c.wait_recv()
-        for c in second[p][3] + second[p][2]:
-            c.start()
+        near, far, third, fourth = second[p]
+        for came, on4, on3 in zip(far, fourth, third):
+            came.wait_recv()
+            on4.start()
+            on3.start()
 
     def arrived(kind):
         for group in second:

time: 53.4 us -> 52.4 us (0.981)
  Pallas kernels: 51.1 us -> 50.4 us
    pallas_call x1, Pallas kernels: 51.1 us -> 50.4 us  [local(): pl.pallas_call(kernel, out_shape=(pltpu.VMEM(draft_tokens.shape, f32), pl...]
where the time goes in v4:
time: 52.4 us; the launch traced here: 52.3 us
  Pallas kernels  50.4 us (96%)
  local copies, waits for them, and re-layouts  1.19 us (2%)
  between operations  0.64 us (1%)
    pallas_call x1, Pallas kernels, local(): pl.pallas_call(kernel, out_shape=(pltpu.VMEM(draft_tokens.shape, f32), pl...  50.4 us
    unnamed x2, local copies, waits for them, and re-layouts  1.19 us

profile of v4, /device:TPU:1, one launch (start us, length us, event | category | flops | bytes accessed | tf_op | source)
XLA Modules:
  0.0 52.3 jit_solution(12653807457548582821)
XLA Ops:
  0.6 50.4 %shard_map.95 = (f32[8,6]{1,0:T(8,128)S(1)}, bf16[48,128]{1,0:T(8,128)(2,1)S(1)}) custom-call(bf16[32,384]{1,0:T(8,128)(2,1)} %bitcast.4, bf16[16,128]{1,0:T(8,128)(2,1)} %bitcast.5, bf16[2048,1024]{1,0:T(8,128)(2,1)} %w_hbm.1, bf16[128,128]{1,0:T(8,128)(2,1)} %bitcast.3, bf16[2048,128]{1,0:T(8,128)(2,1)} %wq_hbm.1, s32[8,6]{1,0:T(8,128)} %tok_ref.1, ...), custom_call_target="tpu_custom_call" | custom-call | tf_op jit(solution)/shard_map/pallas_call | solution.py:302
  51.1 0.6 %copy.12 = f32[8,6]{1,0:T(8,128)} copy(f32[8,6]{1,0:T(8,128)S(1)} %get-tuple-element.2) | data formatting | bytes 384
  51.7 0.6 %copy.13 = bf16[48,128]{1,0:T(8,128)(2,1)} copy(bf16[48,128]{1,0:T(8,128)(2,1)S(1)} %get-tuple-element.3) | data formatting | bytes 24576
